TPU v7x, 32 devices: a whole 2x2x4 slice. The times are simulated.
32 devices in a mesh: tmpl: 8 (over y, x, core), sta: 4 (over z).
Axes of the slice: x: 2, y: 2, z: 4, core: 2. Of those that a mesh axis runs over, the one named last changes fastest.
Arguments:
- window: bfloat16 [300, 1024], P('sta', 'tmpl'), may hold values from -6 to 6
- library: bfloat16 [64, 300, 300], P(None, 'sta'), may hold values from -6 to 6
- library_index: int32 [8], P('tmpl'), may hold values from 0 to 63
- moveout: int32 [8, 300], P('tmpl', 'sta'), may hold values from 0 to 212, as said below
- group_of: int32 [300], P('sta'), may hold values from 0 to 15, never falling along the last dimension, each value on 1 to 32 neighbouring positions
Outputs:
- stacks: bfloat16 [8, 16, 512], P('tmpl', None, 'sta')
Inputs may be any that keep to these rules, and one draw needn't show every extreme that they name: Every row of moveout has some channel at 0 and some channel at 212.
All inputs are finite; a program needn't handle non-finite values.
Results may differ from a plain program's by a relative error of at most 0.01.
Values may be sent and summed in bfloat16 or wider, within the bound.
A program may use at most 128 MiB of HBM per device.

v0:
```python
import functools

import jax
import jax.numpy as jnp
from jax import lax
from jax.experimental import pallas as pl
from jax.experimental.pallas import tpu as pltpu
from jax.sharding import PartitionSpec as P

MAX_SHIFT = 212
GROUPS = 16
EPS = 1e-06
LANES = 128
STEP = 32
SUB = LANES // STEP
SPAN = 4
MESH = pl.DeviceIdType.MESH
F32 = jnp.float32
BF16 = jnp.bfloat16


def iota(shape, dim):
    return lax.broadcasted_iota(jnp.int32, shape, dim)


def dot(a, b):
    return jnp.dot(a, b, preferred_element_type=F32)


def kernel(
    n_tmpl, n_sta, chans, length, rows, depth,
    win_ref, lib_ref, index_ref, move_ref, group_ref, out_ref,
    lib, moves, stations, gathered, counts, samples, taps, bands, aligned, power, corr, partial, arrived,
    row_ref, lib_sem, own_sem, move_sem, group_sem, win_send, win_recv, count_send, count_recv, part_send, part_recv,
):
    mine, station = lax.axis_index("tmpl"), lax.axis_index("sta")
    eights = rows // 8
    owned = out_ref.shape[2] // LANES
    blocks = owned * n_sta

    lib_copy = pltpu.make_async_copy(lib_ref, lib, lib_sem)
    own_copy = pltpu.make_async_copy(win_ref, gathered.at[mine], own_sem)
    move_copy = pltpu.make_async_copy(move_ref, moves, move_sem)
    group_copy = pltpu.make_async_copy(group_ref, stations, group_sem)

    barrier = pltpu.get_barrier_semaphore()
    for d in range(1, n_tmpl):
        peer = lax.rem(mine + d, n_tmpl)
        pl.semaphore_signal(barrier, inc=1, device_id=(peer, station), device_id_type=MESH)
    for d in range(1, n_sta):
        peer = lax.rem(station + d, n_sta)
        pl.semaphore_signal(barrier, inc=1, device_id=(mine, peer), device_id_type=MESH)

    for copy in (group_copy, move_copy, own_copy, lib_copy):
        copy.start()

    row_ref[...] = jnp.full(row_ref.shape, -1, jnp.int32)
    group_copy.wait()
    move_copy.wait()
    row_ref[0:1, 0:chans] = stations[...]
    row_ref[1:2, 0:chans] = moves[...]
    members = jnp.where(iota((GROUPS, LANES), 0) == row_ref[0:1, :], 1.0, 0.0)
    counts[station] = jnp.broadcast_to(jnp.sum(members, axis=1, keepdims=True), (GROUPS, LANES))

    pl.semaphore_wait(barrier, n_tmpl + n_sta - 2)

    def win_copy(d):
        return pltpu.make_async_remote_copy(
            src_ref=win_ref,
            dst_ref=gathered.at[mine],
            send_sem=win_send.at[d],
            recv_sem=win_recv.at[d],
            device_id=(lax.rem(mine + d, n_tmpl), station),
            device_id_type=MESH,
        )

    def win_arrival(d):
        return pltpu.make_async_remote_copy(
            src_ref=win_ref,
            dst_ref=gathered.at[lax.rem(mine - d + n_tmpl, n_tmpl)],
            send_sem=win_send.at[d],
            recv_sem=win_recv.at[d],
            device_id=(lax.rem(mine + d, n_tmpl), station),
            device_id_type=MESH,
        )

    def count_copy(d, slot):
        return pltpu.make_async_remote_copy(
            src_ref=counts.at[station],
            dst_ref=counts.at[slot],
            send_sem=count_send.at[d],
            recv_sem=count_recv.at[d],
            device_id=(mine, lax.rem(station + d, n_sta)),
            device_id_type=MESH,
        )

    def part_copy(d, slot):
        owner = lax.rem(station + d, n_sta)
        return pltpu.make_async_remote_copy(
            src_ref=partial.at[pl.ds(owner * owned, owned)],
            dst_ref=arrived.at[slot],
            send_sem=part_send.at[d],
            recv_sem=part_recv.at[d],
            device_id=(mine, owner),
            device_id_type=MESH,
        )

    for d in range(1, n_tmpl):
        win_copy(d).start()
    for d in range(1, n_sta):
        count_copy(d, station).start()

    lane = iota((rows, LANES), 1)
    sub = iota((rows, LANES), 0)
    moved = jnp.sum(
        jnp.where(lane == sub, row_ref[1:2, :], 0).astype(F32), axis=1, keepdims=True
    ).astype(jnp.int32)
    moved = jnp.broadcast_to(moved, (rows, LANES))
    real = sub < chans
    far = moved >= LANES
    rest = moved & (LANES - 1)
    turn = (lane + rest) & (LANES - 1)
    inside = lane < LANES - rest
    offset = iota((4 * LANES, LANES), 0) - iota((4 * LANES, LANES), 1)
    window_band = jnp.where((offset >= 0) & (offset < length), 1.0, 0.0).astype(BF16)
    row_of = iota((SPAN * SUB * 8, LANES), 0) & 7
    upper_half = row_of >= 8 // 2
    own_lane = (row_of % SUB) * STEP + (iota((SPAN * SUB * 8, LANES), 1) & (STEP - 1))
    members_b = members.astype(BF16)[:, :rows]

    which = index_ref[0]
    spot = iota((rows, 16 * chans), 1)
    take = ((spot >> 4) == iota((rows, 16 * chans), 0)) & ((spot & 15) == (which & 15))
    lib_copy.wait()
    choices = lib[:, which >> 4].reshape(16 * chans, length)
    taps[...] = jnp.zeros(taps.shape, F32)
    taps[:, 0:length] = dot(jnp.where(take, 1.0, 0.0).astype(BF16), choices)
    chosen = taps[...]
    in_taps = iota((rows, depth), 1) < length
    centered = chosen - jnp.sum(chosen, axis=1, keepdims=True) / length
    centered = jnp.where(in_taps, centered, 0.0)
    factor = lax.rsqrt(jnp.sum(centered * centered, axis=1, keepdims=True) / length + EPS)
    taps[...] = (centered * factor).astype(BF16).astype(F32)
    for c in range(rows):
        row = jnp.broadcast_to(taps[c : c + 1, :], (STEP, depth))
        band = pltpu.roll(row, 0, 1, stride=1, stride_axis=0)
        bands[c // 8, STEP * (c % 8) : STEP * (c % 8) + STEP, :] = band.astype(BF16)

    own_copy.wait()
    for d in range(1, n_tmpl):
        win_arrival(d).wait_recv()

    whole = SPAN + 4

    def chunk(step):
        base = step * SPAN
        raw = []
        for b in range(whole):
            samples[b, 0:chans, :] = gathered[base + b].astype(F32)
        for b in range(whole):
            raw.append(jnp.where(real, samples[b], 0.0))
        zero = jnp.zeros((rows, LANES), F32)
        raw.append(zero)
        turned = []
        for b in range(whole):
            value = jnp.where(far, raw[b + 1], raw[b])
            turned.append(jnp.take_along_axis(value, turn, axis=1))
        start = [jnp.where(inside, turned[b], turned[b + 1]) for b in range(whole - 1)]
        for b in range(SPAN + 2):
            views = [start[b]]
            for q in range(1, SUB):
                back = LANES - STEP * q
                views.append(
                    jnp.where(
                        lane < back,
                        pltpu.roll(start[b], back, 1),
                        pltpu.roll(start[b + 1], back, 1),
                    )
                )
            stacked = jnp.concatenate([v.reshape(eights, 8, LANES) for v in views], axis=1)
            aligned[b] = stacked.astype(BF16)
        for b in range(whole - 1):
            power[b] = (start[b] * start[b]).astype(BF16)
        left = jnp.concatenate([power[a : a + SPAN].reshape(SPAN * rows, LANES) for a in range(4)], axis=1)
        inverse = lax.rsqrt(dot(left, window_band) / length + EPS) / length
        inverse = inverse.reshape(SPAN, rows, LANES)
        quarter = iota((SPAN, 8, LANES), 2) // STEP
        for e in range(eights):
            left = jnp.concatenate(
                [aligned[a : a + SPAN, e].reshape(SPAN * SUB * 8, LANES) for a in range(depth // LANES)],
                axis=1,
            )
            crossed = lax.dot_general(
                left, bands[e], (((1,), (1,)), ((), ())), preferred_element_type=F32
            )
            half = jnp.where(upper_half, crossed[:, LANES:], crossed[:, :LANES])
            folded = jnp.take_along_axis(half, own_lane, axis=1).reshape(SPAN, SUB, 8, LANES)
            picked = folded[:, 0]
            for q in range(1, SUB):
                picked = jnp.where(quarter == q, folded[:, q], picked)
            corr[:, 8 * e : 8 * e + 8, :] = picked
        for p in range(SPAN):
            weighted = (corr[p] * inverse[p]).astype(BF16)
            partial[base + p] = dot(members_b, weighted).astype(BF16)

    if blocks == SPAN:
        chunk(0)
    else:

        @pl.loop(0, blocks // SPAN)
        def _(step):
            chunk(step)

    for d in range(1, n_sta):
        part_copy(d, station).start()
    for d in range(1, n_sta):
        count_copy(d, lax.rem(station - d + n_sta, n_sta)).wait_recv()
    total_count = counts[0]
    for s in range(1, n_sta):
        total_count = total_count + counts[s]
    scale = jnp.sqrt(length / total_count)
    arrived[station] = partial[pl.ds(station * owned, owned)]
    for d in range(1, n_sta):
        part_copy(d, lax.rem(station - d + n_sta, n_sta)).wait_recv()
    for b in range(owned):
        total = arrived[0, b].astype(F32)
        for s in range(1, n_sta):
            total = total + arrived[s, b].astype(F32)
        out_ref[0, :, LANES * b : LANES * b + LANES] = (total * scale).astype(BF16)

    for d in range(1, n_tmpl):
        win_copy(d).wait_send()
    for d in range(1, n_sta):
        count_copy(d, station).wait_send()
        part_copy(d, station).wait_send()


def on_device(n_tmpl, n_sta, window, library, library_index, moveout, group_of):
    chans, width = window.shape
    length = library.shape[2]
    lags = width * n_tmpl - length - MAX_SHIFT
    owned = lags // n_sta
    blocks = lags // LANES
    rows = -(-chans // 8) * 8
    depth = -(-(length + STEP - 1) // LANES) * LANES
    by_channel = jnp.transpose(library, (1, 0, 2)).reshape(chans, -1, 16, length)
    vmem = pl.BlockSpec(memory_space=pltpu.VMEM)
    return pl.pallas_call(
        functools.partial(kernel, n_tmpl, n_sta, chans, length, rows, depth),
        out_shape=jax.ShapeDtypeStruct((1, GROUPS, owned), BF16),
        in_specs=[
            pl.BlockSpec(memory_space=pl.ANY),
            pl.BlockSpec(memory_space=pl.ANY),
            pl.BlockSpec(memory_space=pltpu.SMEM),
            pl.BlockSpec(memory_space=pl.ANY),
            pl.BlockSpec(memory_space=pl.ANY),
        ],
        out_specs=vmem,
        scratch_shapes=[
            pltpu.VMEM(by_channel.shape, BF16),
            pltpu.VMEM((1, chans), jnp.int32),
            pltpu.VMEM((1, chans), jnp.int32),
            pltpu.VMEM((n_tmpl, chans, width), BF16),
            pltpu.VMEM((n_sta, GROUPS, LANES), F32),
            pltpu.VMEM((SPAN + 4, rows, LANES), F32),
            pltpu.VMEM((rows, depth), F32),
            pltpu.VMEM((rows // 8, 8 * STEP, depth), BF16),
            pltpu.VMEM((SPAN + 2, rows // 8, 8 * SUB, LANES), BF16),
            pltpu.VMEM((SPAN + 3, rows, LANES), BF16),
            pltpu.VMEM((SPAN, rows, LANES), F32),
            pltpu.VMEM((blocks, GROUPS, LANES), BF16),
            pltpu.VMEM((n_sta, blocks // n_sta, GROUPS, LANES), BF16),
            pltpu.VMEM((8, LANES), jnp.int32),
            pltpu.SemaphoreType.DMA,
            pltpu.SemaphoreType.DMA,
            pltpu.SemaphoreType.DMA,
            pltpu.SemaphoreType.DMA,
            pltpu.SemaphoreType.DMA((n_tmpl,)),
            pltpu.SemaphoreType.DMA((n_tmpl,)),
            pltpu.SemaphoreType.DMA((n_sta,)),
            pltpu.SemaphoreType.DMA((n_sta,)),
            pltpu.SemaphoreType.DMA((n_sta,)),
            pltpu.SemaphoreType.DMA((n_sta,)),
        ],
        compiler_params=pltpu.CompilerParams(
            collective_id=0, has_side_effects=True, vmem_limit_bytes=62 * 1024 * 1024
        ),
    )(window, by_channel, library_index, moveout, group_of.reshape(1, -1))


def solution(mesh):
    in_specs = (P("sta", "tmpl"), P(None, "sta", None), P("tmpl"), P("tmpl", "sta"), P("sta"))
    body = functools.partial(on_device, mesh.shape["tmpl"], mesh.shape["sta"])
    return jax.shard_map(
        body, mesh=mesh, in_specs=in_specs, out_specs=P("tmpl", None, "sta"), check_vma=False
    )
```

profile of v0, /device:TPU:0, one launch (start us, length us, event | category | flops | bytes accessed | tf_op | source)
XLA Modules:
  0.0 16.6 jit_solution(98957019119555676)
XLA Ops:
  0.7 14.6 %shard_map.55 = bf16[1,16,128]{2,1,0:T(8,128)(2,1)} custom-call(bf16[75,128]{1,0:T(8,128)(2,1)} %win_ref.1, bf16[75,4,16,300]{3,2,1,0:T(8,128)(2,1)} %bitcast.4, s32[1]{0:T(128)S(6)} %copy.7.index_ref, s32[1,75]{1,0:T(1,128)} %move_ref.1, s32[1,75]{1,0:T(1,128)} %bitcast.5), custom_call_target="tpu_custom_call" | custom-call | tf_op jit(solution)/shard_map/pallas_call | solution.py:248
  15.3 1.3 %copy.8 = bf16[1,16,128]{2,1,0:T(8,128)(2,1)} copy(bf16[1,16,128]{2,1,0:T(8,128)(2,1)} %shard_map.55) | data formatting | bytes 8192
where the time goes:
time: 16.7 us; the launch traced here: 16.6 us
  Pallas kernels  14.6 us (87%)
  local copies, waits for them, and re-layouts  1.28 us (8%)
  between operations  0.66 us (4%)
    pallas_call x1, Pallas kernels, on_device(): pl.pallas_call(functools.partial(kernel, n_tmpl, n_sta, chans, length, ro...  14.6 us
    unnamed x1, local copies, waits for them, and re-layouts  1.28 us

commit v1 on v0

--- a/solution.py
+++ b/solution.py
@@ -14,6 +14,7 @@
 STEP = 32
 SUB = LANES // STEP
 SPAN = 4
+LIB_COPIES = 5
 MESH = pl.DeviceIdType.MESH
 F32 = jnp.float32
 BF16 = jnp.bfloat16
@@ -30,7 +31,7 @@
 def kernel(
     n_tmpl, n_sta, chans, length, rows, depth,
     win_ref, lib_ref, index_ref, move_ref, group_ref, out_ref,
-    lib, moves, stations, gathered, counts, samples, taps, bands, aligned, power, corr, partial, arrived,
+    lib, moves, stations, gathered, counts, widened, turned, taps, bands, aligned, power, corr, partial, arrived,
     row_ref, lib_sem, own_sem, move_sem, group_sem, win_send, win_recv, count_send, count_recv, part_send, part_recv,
 ):
     mine, station = lax.axis_index("tmpl"), lax.axis_index("sta")
@@ -38,7 +39,11 @@
     owned = out_ref.shape[2] // LANES
     blocks = owned * n_sta
 
-    lib_copy = pltpu.make_async_copy(lib_ref, lib, lib_sem)
+    share = -(-chans // LIB_COPIES)
+    lib_copies = []
+    for k in range(LIB_COPIES):
+        piece = pl.ds(k * share, min(share, chans - k * share))
+        lib_copies.append(pltpu.make_async_copy(lib_ref.at[piece], lib.at[piece], lib_sem.at[k]))
     own_copy = pltpu.make_async_copy(win_ref, gathered.at[mine], own_sem)
     move_copy = pltpu.make_async_copy(move_ref, moves, move_sem)
     group_copy = pltpu.make_async_copy(group_ref, stations, group_sem)
@@ -51,9 +56,54 @@
         peer = lax.rem(station + d, n_sta)
         pl.semaphore_signal(barrier, inc=1, device_id=(mine, peer), device_id_type=MESH)
 
-    for copy in (group_copy, move_copy, own_copy, lib_copy):
+    for copy in [group_copy, move_copy, own_copy] + lib_copies:
         copy.start()
 
+    pl.semaphore_wait(barrier, n_tmpl + n_sta - 2)
+
+    def win_copy(d):
+        return pltpu.make_async_remote_copy(
+            src_ref=win_ref,
+            dst_ref=gathered.at[mine],
+            send_sem=win_send.at[d],
+            recv_sem=win_recv.at[d],
+            device_id=(lax.rem(mine + d, n_tmpl), station),
+            device_id_type=MESH,
+        )
+
+    def win_arrival(d):
+        return pltpu.make_async_remote_copy(
+            src_ref=win_ref,
+            dst_ref=gathered.at[lax.rem(mine - d + n_tmpl, n_tmpl)],
+            send_sem=win_send.at[d],
+            recv_sem=win_recv.at[d],
+            device_id=(lax.rem(mine + d, n_tmpl), station),
+            device_id_type=MESH,
+        )
+
+    def count_copy(d, slot):
+        return pltpu.make_async_remote_copy(
+            src_ref=counts.at[station],
+            dst_ref=counts.at[slot],
+            send_sem=count_send.at[d],
+            recv_sem=count_recv.at[d],
+            device_id=(mine, lax.rem(station + d, n_sta)),
+            device_id_type=MESH,
+        )
+
+    def part_copy(d, slot):
+        owner = lax.rem(station + d, n_sta)
+        return pltpu.make_async_remote_copy(
+            src_ref=partial.at[pl.ds(owner * owned, owned)],
+            dst_ref=arrived.at[slot],
+            send_sem=part_send.at[d],
+            recv_sem=part_recv.at[d],
+            device_id=(mine, owner),
+            device_id_type=MESH,
+        )
+
+    for d in range(1, n_tmpl):
+        win_copy(d).start()
     row_ref[...] = jnp.full(row_ref.shape, -1, jnp.int32)
     group_copy.wait()
     move_copy.wait()
@@ -61,52 +111,6 @@
     row_ref[1:2, 0:chans] = moves[...]
     members = jnp.where(iota((GROUPS, LANES), 0) == row_ref[0:1, :], 1.0, 0.0)
     counts[station] = jnp.broadcast_to(jnp.sum(members, axis=1, keepdims=True), (GROUPS, LANES))
-
-    pl.semaphore_wait(barrier, n_tmpl + n_sta - 2)
-
-    def win_copy(d):
-        return pltpu.make_async_remote_copy(
-            src_ref=win_ref,
-            dst_ref=gathered.at[mine],
-            send_sem=win_send.at[d],
-            recv_sem=win_recv.at[d],
-            device_id=(lax.rem(mine + d, n_tmpl), station),
-            device_id_type=MESH,
-        )
-
-    def win_arrival(d):
-        return pltpu.make_async_remote_copy(
-            src_ref=win_ref,
-            dst_ref=gathered.at[lax.rem(mine - d + n_tmpl, n_tmpl)],
-            send_sem=win_send.at[d],
-            recv_sem=win_recv.at[d],
-            device_id=(lax.rem(mine + d, n_tmpl), station),
-            device_id_type=MESH,
-        )
-
-    def count_copy(d, slot):
-        return pltpu.make_async_remote_copy(
-            src_ref=counts.at[station],
-            dst_ref=counts.at[slot],
-            send_sem=count_send.at[d],
-            recv_sem=count_recv.at[d],
-            device_id=(mine, lax.rem(station + d, n_sta)),
-            device_id_type=MESH,
-        )
-
-    def part_copy(d, slot):
-        owner = lax.rem(station + d, n_sta)
-        return pltpu.make_async_remote_copy(
-            src_ref=partial.at[pl.ds(owner * owned, owned)],
-            dst_ref=arrived.at[slot],
-            send_sem=part_send.at[d],
-            recv_sem=part_recv.at[d],
-            device_id=(mine, owner),
-            device_id_type=MESH,
-        )
-
-    for d in range(1, n_tmpl):
-        win_copy(d).start()
     for d in range(1, n_sta):
         count_copy(d, station).start()
 
@@ -117,10 +121,9 @@
     ).astype(jnp.int32)
     moved = jnp.broadcast_to(moved, (rows, LANES))
     real = sub < chans
-    far = moved >= LANES
-    rest = moved & (LANES - 1)
-    turn = (lane + rest) & (LANES - 1)
-    inside = lane < LANES - rest
+    turns = [(lane + moved + STEP * q) & (LANES - 1) for q in range(SUB)]
+    blocks_on = [(lane + moved + STEP * q) >> 7 for q in range(SUB)]
+    farthest = [(LANES - 1 + MAX_SHIFT + STEP * q) >> 7 for q in range(SUB)]
     offset = iota((4 * LANES, LANES), 0) - iota((4 * LANES, LANES), 1)
     window_band = jnp.where((offset >= 0) & (offset < length), 1.0, 0.0).astype(BF16)
     row_of = iota((SPAN * SUB * 8, LANES), 0) & 7
@@ -131,7 +134,8 @@
     which = index_ref[0]
     spot = iota((rows, 16 * chans), 1)
     take = ((spot >> 4) == iota((rows, 16 * chans), 0)) & ((spot & 15) == (which & 15))
-    lib_copy.wait()
+    for copy in lib_copies:
+        copy.wait()
     choices = lib[:, which >> 4].reshape(16 * chans, length)
     taps[...] = jnp.zeros(taps.shape, F32)
     taps[:, 0:length] = dot(jnp.where(take, 1.0, 0.0).astype(BF16), choices)
@@ -146,41 +150,34 @@
         band = pltpu.roll(row, 0, 1, stride=1, stride_axis=0)
         bands[c // 8, STEP * (c % 8) : STEP * (c % 8) + STEP, :] = band.astype(BF16)
 
+    def turn_block(slot):
+        widened[0:chans, :] = gathered[slot].astype(F32)
+        values = jnp.where(real, widened[...], 0.0)
+        for q in range(SUB):
+            turned[q, slot] = jnp.take_along_axis(values, turns[q], axis=1)
+
     own_copy.wait()
+    turn_block(mine)
     for d in range(1, n_tmpl):
         win_arrival(d).wait_recv()
+        turn_block(lax.rem(mine - d + n_tmpl, n_tmpl))
 
     whole = SPAN + 4
 
     def chunk(step):
         base = step * SPAN
-        raw = []
-        for b in range(whole):
-            samples[b, 0:chans, :] = gathered[base + b].astype(F32)
-        for b in range(whole):
-            raw.append(jnp.where(real, samples[b], 0.0))
-        zero = jnp.zeros((rows, LANES), F32)
-        raw.append(zero)
-        turned = []
-        for b in range(whole):
-            value = jnp.where(far, raw[b + 1], raw[b])
-            turned.append(jnp.take_along_axis(value, turn, axis=1))
-        start = [jnp.where(inside, turned[b], turned[b + 1]) for b in range(whole - 1)]
-        for b in range(SPAN + 2):
-            views = [start[b]]
-            for q in range(1, SUB):
-                back = LANES - STEP * q
-                views.append(
-                    jnp.where(
-                        lane < back,
-                        pltpu.roll(start[b], back, 1),
-                        pltpu.roll(start[b + 1], back, 1),
-                    )
-                )
-            stacked = jnp.concatenate([v.reshape(eights, 8, LANES) for v in views], axis=1)
-            aligned[b] = stacked.astype(BF16)
         for b in range(whole - 1):
-            power[b] = (start[b] * start[b]).astype(BF16)
+            views = []
+            for q in range(SUB if b < SPAN + 2 else 1):
+                value = turned[q, base + b]
+                for ahead in range(1, farthest[q] + 1):
+                    if b + ahead < whole:
+                        value = jnp.where(blocks_on[q] == ahead, turned[q, base + b + ahead], value)
+                views.append(value)
+            power[b] = (views[0] * views[0]).astype(BF16)
+            if b < SPAN + 2:
+                stacked = jnp.concatenate([v.reshape(eights, 8, LANES) for v in views], axis=1)
+                aligned[b] = stacked.astype(BF16)
         left = jnp.concatenate([power[a : a + SPAN].reshape(SPAN * rows, LANES) for a in range(4)], axis=1)
         inverse = lax.rsqrt(dot(left, window_band) / length + EPS) / length
         inverse = inverse.reshape(SPAN, rows, LANES)
@@ -262,7 +259,8 @@
             pltpu.VMEM((1, chans), jnp.int32),
             pltpu.VMEM((n_tmpl, chans, width), BF16),
             pltpu.VMEM((n_sta, GROUPS, LANES), F32),
-            pltpu.VMEM((SPAN + 4, rows, LANES), F32),
+            pltpu.VMEM((rows, LANES), F32),
+            pltpu.VMEM((SUB, n_tmpl, rows, LANES), F32),
             pltpu.VMEM((rows, depth), F32),
             pltpu.VMEM((rows // 8, 8 * STEP, depth), BF16),
             pltpu.VMEM((SPAN + 2, rows // 8, 8 * SUB, LANES), BF16),
@@ -271,7 +269,7 @@
             pltpu.VMEM((blocks, GROUPS, LANES), BF16),
             pltpu.VMEM((n_sta, blocks // n_sta, GROUPS, LANES), BF16),
             pltpu.VMEM((8, LANES), jnp.int32),
-            pltpu.SemaphoreType.DMA,
+            pltpu.SemaphoreType.DMA((LIB_COPIES,)),
             pltpu.SemaphoreType.DMA,
             pltpu.SemaphoreType.DMA,
             pltpu.SemaphoreType.DMA,
@@ -283,7 +281,7 @@
             pltpu.SemaphoreType.DMA((n_sta,)),
         ],
         compiler_params=pltpu.CompilerParams(
-            collective_id=0, has_side_effects=True, vmem_limit_bytes=62 * 1024 * 1024
+            collective_id=0, has_side_effects=True, vmem_limit_bytes=56 * 1024 * 1024
         ),
     )(window, by_channel, library_index, moveout, group_of.reshape(1, -1))
 

time: 16.7 us -> 17.2 us (1.030)
  Pallas kernels: 14.6 us -> 15 us
    pallas_call x1, Pallas kernels: 14.6 us -> 15 us  [on_device(): pl.pallas_call(functools.partial(kernel, n_tmpl, n_sta, chans, length, ro...]
where the time goes in v1:
time: 17.2 us; the launch traced here: 17 us
  Pallas kernels  15 us (87%)
  local copies, waits for them, and re-layouts  1.28 us (7%)
  between operations  0.66 us (4%)
    pallas_call x1, Pallas kernels, on_device(): pl.pallas_call(functools.partial(kernel, n_tmpl, n_sta, chans, length, ro...  15 us
    unnamed x1, local copies, waits for them, and re-layouts  1.28 us

profile of v1, /device:TPU:0, one launch (start us, length us, event | category | flops | bytes accessed | tf_op | source)
XLA Modules:
  0.0 17.0 jit_solution(688943030854959306)
XLA Ops:
  0.7 15.0 %shard_map.55 = bf16[1,16,128]{2,1,0:T(8,128)(2,1)} custom-call(bf16[75,128]{1,0:T(8,128)(2,1)} %win_ref.1, bf16[75,4,16,300]{3,2,1,0:T(8,128)(2,1)} %bitcast.4, s32[1]{0:T(128)S(6)} %copy.7.index_ref, s32[1,75]{1,0:T(1,128)} %move_ref.1, s32[1,75]{1,0:T(1,128)} %bitcast.5), custom_call_target="tpu_custom_call" | custom-call | tf_op jit(solution)/shard_map/pallas_call | solution.py:245
  15.7 1.3 %copy.8 = bf16[1,16,128]{2,1,0:T(8,128)(2,1)} copy(bf16[1,16,128]{2,1,0:T(8,128)(2,1)} %shard_map.55) | data formatting | bytes 8192

commit v2 on v1

--- a/solution.py
+++ b/solution.py
@@ -31,7 +31,7 @@
 def kernel(
     n_tmpl, n_sta, chans, length, rows, depth,
     win_ref, lib_ref, index_ref, move_ref, group_ref, out_ref,
-    lib, moves, stations, gathered, counts, widened, turned, taps, bands, aligned, power, corr, partial, arrived,
+    lib, moves, stations, gathered, counts, widened, turned, ahead_of, taps, bands, power, corr, partial, arrived,
     row_ref, lib_sem, own_sem, move_sem, group_sem, win_send, win_recv, count_send, count_recv, part_send, part_recv,
 ):
     mine, station = lax.axis_index("tmpl"), lax.axis_index("sta")
@@ -122,43 +122,51 @@
     moved = jnp.broadcast_to(moved, (rows, LANES))
     real = sub < chans
     turns = [(lane + moved + STEP * q) & (LANES - 1) for q in range(SUB)]
-    blocks_on = [(lane + moved + STEP * q) >> 7 for q in range(SUB)]
+    for q in range(SUB):
+        ahead_of[q] = ((lane + moved + STEP * q) >> 7).reshape(eights, 8, LANES)
     farthest = [(LANES - 1 + MAX_SHIFT + STEP * q) >> 7 for q in range(SUB)]
     offset = iota((4 * LANES, LANES), 0) - iota((4 * LANES, LANES), 1)
     window_band = jnp.where((offset >= 0) & (offset < length), 1.0, 0.0).astype(BF16)
-    row_of = iota((SPAN * SUB * 8, LANES), 0) & 7
-    upper_half = row_of >= 8 // 2
-    own_lane = (row_of % SUB) * STEP + (iota((SPAN * SUB * 8, LANES), 1) & (STEP - 1))
+    upper_half = iota((1, 8, LANES), 1) >= 8 // 2
+    own_lane = (iota((1, 8, LANES), 1) % SUB) * STEP + (iota((1, 8, LANES), 2) & (STEP - 1))
+    own_lane = jnp.broadcast_to(own_lane, (SPAN * SUB, 8, LANES)).reshape(SPAN * SUB * 8, LANES)
     members_b = members.astype(BF16)[:, :rows]
 
     which = index_ref[0]
-    spot = iota((rows, 16 * chans), 1)
-    take = ((spot >> 4) == iota((rows, 16 * chans), 0)) & ((spot & 15) == (which & 15))
+    take = ((iota((8, LANES), 1) >> 4) == iota((8, LANES), 0)) & ((iota((8, LANES), 1) & 15) == (which & 15))
+    take = jnp.where(take, 1.0, 0.0).astype(BF16)
+    taps[...] = jnp.zeros(taps.shape, F32)
+    lib[chans:rows] = jnp.zeros((rows - chans,) + lib.shape[1:], BF16)
     for copy in lib_copies:
         copy.wait()
-    choices = lib[:, which >> 4].reshape(16 * chans, length)
-    taps[...] = jnp.zeros(taps.shape, F32)
-    taps[:, 0:length] = dot(jnp.where(take, 1.0, 0.0).astype(BF16), choices)
-    chosen = taps[...]
+    for e in range(eights):
+        choices = lib[8 * e : 8 * e + 8, which >> 4].reshape(LANES, length)
+        taps[e, :, 0:length] = dot(take, choices)
+    chosen = taps[...].reshape(rows, depth)
     in_taps = iota((rows, depth), 1) < length
     centered = chosen - jnp.sum(chosen, axis=1, keepdims=True) / length
     centered = jnp.where(in_taps, centered, 0.0)
     factor = lax.rsqrt(jnp.sum(centered * centered, axis=1, keepdims=True) / length + EPS)
-    taps[...] = (centered * factor).astype(BF16).astype(F32)
-    for c in range(rows):
-        row = jnp.broadcast_to(taps[c : c + 1, :], (STEP, depth))
-        band = pltpu.roll(row, 0, 1, stride=1, stride_axis=0)
-        bands[c // 8, STEP * (c % 8) : STEP * (c % 8) + STEP, :] = band.astype(BF16)
+    taps[...] = (centered * factor).astype(BF16).astype(F32).reshape(eights, 8, depth)
+
+    @pl.loop(0, eights)
+    def _(e):
+        for c in range(8):
+            row = jnp.broadcast_to(taps[e, c : c + 1, :], (STEP, depth))
+            band = pltpu.roll(row, 0, 1, stride=1, stride_axis=0)
+            bands[e, STEP * c : STEP * c + STEP, :] = band.astype(BF16)
 
     def turn_block(slot):
         widened[0:chans, :] = gathered[slot].astype(F32)
         values = jnp.where(real, widened[...], 0.0)
         for q in range(SUB):
-            turned[q, slot] = jnp.take_along_axis(values, turns[q], axis=1)
+            turned[q, slot] = jnp.take_along_axis(values, turns[q], axis=1).reshape(eights, 8, LANES)
 
     own_copy.wait()
     turn_block(mine)
-    for d in range(1, n_tmpl):
+
+    @pl.loop(1, n_tmpl)
+    def _(d):
         win_arrival(d).wait_recv()
         turn_block(lax.rem(mine - d + n_tmpl, n_tmpl))
 
@@ -166,38 +174,44 @@
 
     def chunk(step):
         base = step * SPAN
-        for b in range(whole - 1):
-            views = []
-            for q in range(SUB if b < SPAN + 2 else 1):
-                value = turned[q, base + b]
-                for ahead in range(1, farthest[q] + 1):
-                    if b + ahead < whole:
-                        value = jnp.where(blocks_on[q] == ahead, turned[q, base + b + ahead], value)
-                views.append(value)
-            power[b] = (views[0] * views[0]).astype(BF16)
-            if b < SPAN + 2:
-                stacked = jnp.concatenate([v.reshape(eights, 8, LANES) for v in views], axis=1)
-                aligned[b] = stacked.astype(BF16)
-        left = jnp.concatenate([power[a : a + SPAN].reshape(SPAN * rows, LANES) for a in range(4)], axis=1)
-        inverse = lax.rsqrt(dot(left, window_band) / length + EPS) / length
-        inverse = inverse.reshape(SPAN, rows, LANES)
         quarter = iota((SPAN, 8, LANES), 2) // STEP
-        for e in range(eights):
+
+        @pl.loop(0, eights, unroll=2)
+        def _(e):
+            pieces = []
+            for b in range(whole - 1):
+                views = []
+                for q in range(SUB if b < SPAN + 2 else 1):
+                    value = turned[q, base + b, e]
+                    for ahead in range(1, farthest[q] + 1):
+                        if b + ahead < whole:
+                            value = jnp.where(ahead_of[q, e] == ahead, turned[q, base + b + ahead, e], value)
+                    views.append(value)
+                power[b, e] = views[0] * views[0]
+                if b < SPAN + 2:
+                    pieces.append(jnp.concatenate(views, axis=0).astype(BF16))
             left = jnp.concatenate(
-                [aligned[a : a + SPAN, e].reshape(SPAN * SUB * 8, LANES) for a in range(depth // LANES)],
-                axis=1,
+                [jnp.concatenate(pieces[a : a + SPAN], axis=0) for a in range(depth // LANES)], axis=1
             )
             crossed = lax.dot_general(
                 left, bands[e], (((1,), (1,)), ((), ())), preferred_element_type=F32
-            )
-            half = jnp.where(upper_half, crossed[:, LANES:], crossed[:, :LANES])
-            folded = jnp.take_along_axis(half, own_lane, axis=1).reshape(SPAN, SUB, 8, LANES)
+            ).reshape(SPAN * SUB, 8, 8 * STEP)
+            half = jnp.where(upper_half, crossed[:, :, LANES:], crossed[:, :, :LANES])
+            folded = jnp.take_along_axis(half.reshape(SPAN * SUB * 8, LANES), own_lane, axis=1)
+            folded = folded.reshape(SPAN, SUB, 8, LANES)
             picked = folded[:, 0]
             for q in range(1, SUB):
                 picked = jnp.where(quarter == q, folded[:, q], picked)
-            corr[:, 8 * e : 8 * e + 8, :] = picked
+            corr[:, e] = picked
+
+        squares = [power[b].reshape(rows, LANES).astype(BF16) for b in range(whole - 1)]
+        left = jnp.concatenate(
+            [jnp.concatenate(squares[a : a + SPAN], axis=0) for a in range(4)], axis=1
+        )
+        inverse = lax.rsqrt(dot(left, window_band) / length + EPS) / length
+        inverse = inverse.reshape(SPAN, rows, LANES)
         for p in range(SPAN):
-            weighted = (corr[p] * inverse[p]).astype(BF16)
+            weighted = (corr[p].reshape(rows, LANES) * inverse[p]).astype(BF16)
             partial[base + p] = dot(members_b, weighted).astype(BF16)
 
     if blocks == SPAN:
@@ -244,28 +258,28 @@
     vmem = pl.BlockSpec(memory_space=pltpu.VMEM)
     return pl.pallas_call(
         functools.partial(kernel, n_tmpl, n_sta, chans, length, rows, depth),
-        out_shape=jax.ShapeDtypeStruct((1, GROUPS, owned), BF16),
+        out_shape=pltpu.VMEM((1, GROUPS, owned), BF16),
         in_specs=[
-            pl.BlockSpec(memory_space=pl.ANY),
-            pl.BlockSpec(memory_space=pl.ANY),
+            pl.BlockSpec(memory_space=pltpu.HBM),
+            pl.BlockSpec(memory_space=pltpu.HBM),
             pl.BlockSpec(memory_space=pltpu.SMEM),
-            pl.BlockSpec(memory_space=pl.ANY),
-            pl.BlockSpec(memory_space=pl.ANY),
+            pl.BlockSpec(memory_space=pltpu.HBM),
+            pl.BlockSpec(memory_space=pltpu.HBM),
         ],
         out_specs=vmem,
         scratch_shapes=[
-            pltpu.VMEM(by_channel.shape, BF16),
+            pltpu.VMEM((rows,) + by_channel.shape[1:], BF16),
             pltpu.VMEM((1, chans), jnp.int32),
             pltpu.VMEM((1, chans), jnp.int32),
             pltpu.VMEM((n_tmpl, chans, width), BF16),
             pltpu.VMEM((n_sta, GROUPS, LANES), F32),
             pltpu.VMEM((rows, LANES), F32),
-            pltpu.VMEM((SUB, n_tmpl, rows, LANES), F32),
-            pltpu.VMEM((rows, depth), F32),
+            pltpu.VMEM((SUB, n_tmpl, rows // 8, 8, LANES), F32),
+            pltpu.VMEM((SUB, rows // 8, 8, LANES), jnp.int32),
+            pltpu.VMEM((rows // 8, 8, depth), F32),
             pltpu.VMEM((rows // 8, 8 * STEP, depth), BF16),
-            pltpu.VMEM((SPAN + 2, rows // 8, 8 * SUB, LANES), BF16),
-            pltpu.VMEM((SPAN + 3, rows, LANES), BF16),
-            pltpu.VMEM((SPAN, rows, LANES), F32),
+            pltpu.VMEM((SPAN + 3, rows // 8, 8, LANES), F32),
+            pltpu.VMEM((SPAN, rows // 8, 8, LANES), F32),
             pltpu.VMEM((blocks, GROUPS, LANES), BF16),
             pltpu.VMEM((n_sta, blocks // n_sta, GROUPS, LANES), BF16),
             pltpu.VMEM((8, LANES), jnp.int32),
@@ -281,7 +295,7 @@
             pltpu.SemaphoreType.DMA((n_sta,)),
         ],
         compiler_params=pltpu.CompilerParams(
-            collective_id=0, has_side_effects=True, vmem_limit_bytes=56 * 1024 * 1024
+            collective_id=0, has_side_effects=True, vmem_limit_bytes=52 * 1024 * 1024
         ),
     )(window, by_channel, library_index, moveout, group_of.reshape(1, -1))
 

time: 17.2 us -> 18.7 us (1.087)
  local copies, waits for them, and re-layouts: 1.28 us -> 2.63 us
  Pallas kernels: 15 us -> 15.2 us
    unnamed x1 -> x7, local copies, waits for them, and re-layouts: 1.28 us -> 2.63 us
where the time goes in v2:
time: 18.7 us; the launch traced here: 18.5 us
  Pallas kernels  15.2 us (81%)
  local copies, waits for them, and re-layouts  2.63 us (14%)
  between operations  0.67 us (4%)
    pallas_call x1, Pallas kernels, on_device(): pl.pallas_call(functools.partial(kernel, n_tmpl, n_sta, chans, length, ro...  15.2 us
    unnamed x7, local copies, waits for them, and re-layouts  2.63 us

profile of v2, /device:TPU:0, one launch (start us, length us, event | category | flops | bytes accessed | tf_op | source)
XLA Modules:
  0.0 18.5 jit_solution(11004123440018888831)
XLA Ops:
  0.7 0.0 copy-start
  0.7 0.7 %copy-done = bf16[75,128]{1,0:T(8,128)(2,1)S(1)} copy-done((bf16[75,128]{1,0:T(8,128)(2,1)S(1)}, bf16[75,128]{1,0:T(8,128)(2,1)}, u32[]{:S(2)}) %copy-start) | copy-done | bytes 19224
  1.4 0.0 copy-start.1
  1.4 0.7 %copy-done.1 = s32[1,75]{1,0:T(1,128)S(1)} copy-done((s32[1,75]{1,0:T(1,128)S(1)}, s32[1,75]{1,0:T(1,128)}, u32[]{:S(2)}) %copy-start.1) | copy-done | bytes 324
  2.0 0.0 copy-start.2
  2.0 0.7 %copy-done.2 = s32[75]{0:T(128)S(1)} copy-done((s32[75]{0:T(128)S(1)}, s32[75]{0:T(128)}, u32[]{:S(2)}) %copy-start.2) | copy-done | bytes 324
  2.7 15.2 %shard_map.55 = bf16[1,16,128]{2,1,0:T(8,128)(2,1)S(1)} custom-call(bf16[75,128]{1,0:T(8,128)(2,1)S(1)} %copy-done, bf16[75,4,16,300]{3,2,1,0:T(8,128)(2,1)} %bitcast.5, s32[1]{0:T(128)S(6)} %copy.8.index_ref, s32[1,75]{1,0:T(1,128)S(1)} %copy-done.1, s32[1,75]{1,0:T(1,128)S(1)} %bitcast.4), custom_call_target="tpu_custom_call" | custom-call | tf_op jit(solution)/shard_map/pallas_call | solution.py:259
  17.9 0.6 %copy.7 = bf16[1,16,128]{2,1,0:T(8,128)(2,1)} copy(bf16[1,16,128]{2,1,0:T(8,128)(2,1)S(1)} %shard_map.55) | data formatting | bytes 8192
Async XLA Ops:
  0.7 0.7 %copy-start = (bf16[75,128]{1,0:T(8,128)(2,1)S(1)}, bf16[75,128]{1,0:T(8,128)(2,1)}, u32[]{:S(2)}) copy-start(bf16[75,128]{1,0:T(8,128)(2,1)} %win_ref.1) | copy-start | bytes 57604
  1.4 0.7 %copy-start.1 = (s32[1,75]{1,0:T(1,128)S(1)}, s32[1,75]{1,0:T(1,128)}, u32[]{:S(2)}) copy-start(s32[1,75]{1,0:T(1,128)} %move_ref.1) | copy-start | bytes 904
  2.0 0.7 %copy-start.2 = (s32[75]{0:T(128)S(1)}, s32[75]{0:T(128)}, u32[]{:S(2)}) copy-start(s32[75]{0:T(128)} %param.9) | copy-start | bytes 904

commit v3 on v0

--- a/solution.py
+++ b/solution.py
@@ -38,7 +38,7 @@
     owned = out_ref.shape[2] // LANES
     blocks = owned * n_sta
 
-    lib_copy = pltpu.make_async_copy(lib_ref, lib, lib_sem)
+    lib_copy = pltpu.make_async_copy(lib_ref, lib.at[pl.ds(0, chans)], lib_sem)
     own_copy = pltpu.make_async_copy(win_ref, gathered.at[mine], own_sem)
     move_copy = pltpu.make_async_copy(move_ref, moves, move_sem)
     group_copy = pltpu.make_async_copy(group_ref, stations, group_sem)
@@ -53,14 +53,6 @@
 
     for copy in (group_copy, move_copy, own_copy, lib_copy):
         copy.start()
-
-    row_ref[...] = jnp.full(row_ref.shape, -1, jnp.int32)
-    group_copy.wait()
-    move_copy.wait()
-    row_ref[0:1, 0:chans] = stations[...]
-    row_ref[1:2, 0:chans] = moves[...]
-    members = jnp.where(iota((GROUPS, LANES), 0) == row_ref[0:1, :], 1.0, 0.0)
-    counts[station] = jnp.broadcast_to(jnp.sum(members, axis=1, keepdims=True), (GROUPS, LANES))
 
     pl.semaphore_wait(barrier, n_tmpl + n_sta - 2)
 
@@ -107,6 +99,13 @@
 
     for d in range(1, n_tmpl):
         win_copy(d).start()
+    row_ref[...] = jnp.full(row_ref.shape, -1, jnp.int32)
+    group_copy.wait()
+    move_copy.wait()
+    row_ref[0:1, 0:chans] = stations[...]
+    row_ref[1:2, 0:chans] = moves[...]
+    members = jnp.where(iota((GROUPS, LANES), 0) == row_ref[0:1, :], 1.0, 0.0)
+    counts[station] = jnp.broadcast_to(jnp.sum(members, axis=1, keepdims=True), (GROUPS, LANES))
     for d in range(1, n_sta):
         count_copy(d, station).start()
 
@@ -123,18 +122,21 @@
     inside = lane < LANES - rest
     offset = iota((4 * LANES, LANES), 0) - iota((4 * LANES, LANES), 1)
     window_band = jnp.where((offset >= 0) & (offset < length), 1.0, 0.0).astype(BF16)
-    row_of = iota((SPAN * SUB * 8, LANES), 0) & 7
-    upper_half = row_of >= 8 // 2
-    own_lane = (row_of % SUB) * STEP + (iota((SPAN * SUB * 8, LANES), 1) & (STEP - 1))
+    own = iota((8, LANES), 0)
+    upper_half = own >= 8 // 2
+    own = own % SUB
+    quarter = iota((8, LANES), 1) // STEP
     members_b = members.astype(BF16)[:, :rows]
 
     which = index_ref[0]
-    spot = iota((rows, 16 * chans), 1)
-    take = ((spot >> 4) == iota((rows, 16 * chans), 0)) & ((spot & 15) == (which & 15))
+    take = ((iota((8, LANES), 1) >> 4) == iota((8, LANES), 0)) & ((iota((8, LANES), 1) & 15) == (which & 15))
+    take = jnp.where(take, 1.0, 0.0).astype(BF16)
+    taps[...] = jnp.zeros(taps.shape, F32)
+    lib[chans:rows] = jnp.zeros((rows - chans,) + lib.shape[1:], BF16)
     lib_copy.wait()
-    choices = lib[:, which >> 4].reshape(16 * chans, length)
-    taps[...] = jnp.zeros(taps.shape, F32)
-    taps[:, 0:length] = dot(jnp.where(take, 1.0, 0.0).astype(BF16), choices)
+    for e in range(eights):
+        choices = lib[8 * e : 8 * e + 8, which >> 4].reshape(LANES, length)
+        taps[8 * e : 8 * e + 8, 0:length] = dot(take, choices)
     chosen = taps[...]
     in_taps = iota((rows, depth), 1) < length
     centered = chosen - jnp.sum(chosen, axis=1, keepdims=True) / length
@@ -166,17 +168,14 @@
             value = jnp.where(far, raw[b + 1], raw[b])
             turned.append(jnp.take_along_axis(value, turn, axis=1))
         start = [jnp.where(inside, turned[b], turned[b + 1]) for b in range(whole - 1)]
+        rolled = [
+            [start[b]] + [pltpu.roll(start[b], LANES - STEP * q, 1) for q in range(1, SUB)]
+            for b in range(whole - 1)
+        ]
         for b in range(SPAN + 2):
             views = [start[b]]
             for q in range(1, SUB):
-                back = LANES - STEP * q
-                views.append(
-                    jnp.where(
-                        lane < back,
-                        pltpu.roll(start[b], back, 1),
-                        pltpu.roll(start[b + 1], back, 1),
-                    )
-                )
+                views.append(jnp.where(lane < LANES - STEP * q, rolled[b][q], rolled[b + 1][q]))
             stacked = jnp.concatenate([v.reshape(eights, 8, LANES) for v in views], axis=1)
             aligned[b] = stacked.astype(BF16)
         for b in range(whole - 1):
@@ -184,7 +183,6 @@
         left = jnp.concatenate([power[a : a + SPAN].reshape(SPAN * rows, LANES) for a in range(4)], axis=1)
         inverse = lax.rsqrt(dot(left, window_band) / length + EPS) / length
         inverse = inverse.reshape(SPAN, rows, LANES)
-        quarter = iota((SPAN, 8, LANES), 2) // STEP
         for e in range(eights):
             left = jnp.concatenate(
                 [aligned[a : a + SPAN, e].reshape(SPAN * SUB * 8, LANES) for a in range(depth // LANES)],
@@ -193,12 +191,23 @@
             crossed = lax.dot_general(
                 left, bands[e], (((1,), (1,)), ((), ())), preferred_element_type=F32
             )
-            half = jnp.where(upper_half, crossed[:, LANES:], crossed[:, :LANES])
-            folded = jnp.take_along_axis(half, own_lane, axis=1).reshape(SPAN, SUB, 8, LANES)
-            picked = folded[:, 0]
-            for q in range(1, SUB):
-                picked = jnp.where(quarter == q, folded[:, q], picked)
-            corr[:, 8 * e : 8 * e + 8, :] = picked
+            for p in range(SPAN):
+                halves = []
+                for q in range(SUB):
+                    at = (p * SUB + q) * 8
+                    halves.append(
+                        jnp.where(upper_half, crossed[at : at + 8, LANES:], crossed[at : at + 8, :LANES])
+                    )
+                for r in range(SUB):
+                    value = halves[r]
+                    for c in range(1, SUB):
+                        value = jnp.where(own == c, halves[(r + c) % SUB], value)
+                    if r == 0:
+                        picked = value
+                    else:
+                        value = pltpu.roll(value, STEP * r, 1)
+                        picked = jnp.where(quarter == (own + r) % SUB, value, picked)
+                corr[p, 8 * e : 8 * e + 8, :] = picked
         for p in range(SPAN):
             weighted = (corr[p] * inverse[p]).astype(BF16)
             partial[base + p] = dot(members_b, weighted).astype(BF16)
@@ -247,7 +256,7 @@
     vmem = pl.BlockSpec(memory_space=pltpu.VMEM)
     return pl.pallas_call(
         functools.partial(kernel, n_tmpl, n_sta, chans, length, rows, depth),
-        out_shape=jax.ShapeDtypeStruct((1, GROUPS, owned), BF16),
+        out_shape=pltpu.VMEM((1, GROUPS, owned), BF16),
         in_specs=[
             pl.BlockSpec(memory_space=pl.ANY),
             pl.BlockSpec(memory_space=pl.ANY),
@@ -257,7 +266,7 @@
         ],
         out_specs=vmem,
         scratch_shapes=[
-            pltpu.VMEM(by_channel.shape, BF16),
+            pltpu.VMEM((rows,) + by_channel.shape[1:], BF16),
             pltpu.VMEM((1, chans), jnp.int32),
             pltpu.VMEM((1, chans), jnp.int32),
             pltpu.VMEM((n_tmpl, chans, width), BF16),
@@ -283,7 +292,7 @@
             pltpu.SemaphoreType.DMA((n_sta,)),
         ],
         compiler_params=pltpu.CompilerParams(
-            collective_id=0, has_side_effects=True, vmem_limit_bytes=62 * 1024 * 1024
+            collective_id=0, has_side_effects=True, vmem_limit_bytes=56 * 1024 * 1024
         ),
     )(window, by_channel, library_index, moveout, group_of.reshape(1, -1))
 

time: 16.7 us -> 15.5 us (0.928)
  local copies, waits for them, and re-layouts: 1.28 us -> 0.6 us
  Pallas kernels: 14.6 us -> 14.1 us
    unnamed x1, local copies, waits for them, and re-layouts: 1.28 us -> 0.6 us
    pallas_call x1, Pallas kernels: 14.6 us -> 14.1 us  [on_device(): pl.pallas_call(functools.partial(kernel, n_tmpl, n_sta, chans, length, ro...]
where the time goes in v3:
time: 15.5 us; the launch traced here: 15.3 us
  Pallas kernels  14.1 us (91%)
  between operations  0.66 us (4%)
  local copies, waits for them, and re-layouts  0.6 us (4%)
    pallas_call x1, Pallas kernels, on_device(): pl.pallas_call(functools.partial(kernel, n_tmpl, n_sta, chans, length, ro...  14.1 us
    unnamed x1, local copies, waits for them, and re-layouts  0.6 us

profile of v3, /device:TPU:0, one launch (start us, length us, event | category | flops | bytes accessed | tf_op | source)
XLA Modules:
  0.0 15.3 jit_solution(2192994609452178927)
XLA Ops:
  0.7 14.1 %shard_map.55 = bf16[1,16,128]{2,1,0:T(8,128)(2,1)S(1)} custom-call(bf16[75,128]{1,0:T(8,128)(2,1)} %win_ref.1, bf16[75,4,16,300]{3,2,1,0:T(8,128)(2,1)} %bitcast.4, s32[1]{0:T(128)S(6)} %copy.8.index_ref, s32[1,75]{1,0:T(1,128)} %move_ref.1, s32[1,75]{1,0:T(1,128)} %bitcast.5), custom_call_target="tpu_custom_call" | custom-call | tf_op jit(solution)/shard_map/pallas_call | solution.py:257
  14.7 0.6 %copy.7 = bf16[1,16,128]{2,1,0:T(8,128)(2,1)} copy(bf16[1,16,128]{2,1,0:T(8,128)(2,1)S(1)} %shard_map.55) | data formatting | bytes 8192

commit v4 on v3

--- a/solution.py
+++ b/solution.py
@@ -14,6 +14,7 @@
 STEP = 32
 SUB = LANES // STEP
 SPAN = 4
+LIB_COPIES = 5
 MESH = pl.DeviceIdType.MESH
 F32 = jnp.float32
 BF16 = jnp.bfloat16
@@ -38,7 +39,11 @@
     owned = out_ref.shape[2] // LANES
     blocks = owned * n_sta
 
-    lib_copy = pltpu.make_async_copy(lib_ref, lib.at[pl.ds(0, chans)], lib_sem)
+    share = -(-chans // LIB_COPIES)
+    lib_copies = []
+    for k in range(LIB_COPIES):
+        piece = pl.ds(k * share, min(share, chans - k * share))
+        lib_copies.append(pltpu.make_async_copy(lib_ref.at[piece], lib.at[piece], lib_sem.at[k]))
     own_copy = pltpu.make_async_copy(win_ref, gathered.at[mine], own_sem)
     move_copy = pltpu.make_async_copy(move_ref, moves, move_sem)
     group_copy = pltpu.make_async_copy(group_ref, stations, group_sem)
@@ -51,7 +56,7 @@
         peer = lax.rem(station + d, n_sta)
         pl.semaphore_signal(barrier, inc=1, device_id=(mine, peer), device_id_type=MESH)
 
-    for copy in (group_copy, move_copy, own_copy, lib_copy):
+    for copy in [group_copy, move_copy, own_copy] + lib_copies:
         copy.start()
 
     pl.semaphore_wait(barrier, n_tmpl + n_sta - 2)
@@ -133,7 +138,8 @@
     take = jnp.where(take, 1.0, 0.0).astype(BF16)
     taps[...] = jnp.zeros(taps.shape, F32)
     lib[chans:rows] = jnp.zeros((rows - chans,) + lib.shape[1:], BF16)
-    lib_copy.wait()
+    for copy in lib_copies:
+        copy.wait()
     for e in range(eights):
         choices = lib[8 * e : 8 * e + 8, which >> 4].reshape(LANES, length)
         taps[8 * e : 8 * e + 8, 0:length] = dot(take, choices)
@@ -149,8 +155,11 @@
         bands[c // 8, STEP * (c % 8) : STEP * (c % 8) + STEP, :] = band.astype(BF16)
 
     own_copy.wait()
+    samples[mine, 0:chans, :] = gathered[mine].astype(F32)
     for d in range(1, n_tmpl):
         win_arrival(d).wait_recv()
+        slot = lax.rem(mine - d + n_tmpl, n_tmpl)
+        samples[slot, 0:chans, :] = gathered[slot].astype(F32)
 
     whole = SPAN + 4
 
@@ -158,9 +167,7 @@
         base = step * SPAN
         raw = []
         for b in range(whole):
-            samples[b, 0:chans, :] = gathered[base + b].astype(F32)
-        for b in range(whole):
-            raw.append(jnp.where(real, samples[b], 0.0))
+            raw.append(jnp.where(real, samples[base + b], 0.0))
         zero = jnp.zeros((rows, LANES), F32)
         raw.append(zero)
         turned = []
@@ -271,7 +278,7 @@
             pltpu.VMEM((1, chans), jnp.int32),
             pltpu.VMEM((n_tmpl, chans, width), BF16),
             pltpu.VMEM((n_sta, GROUPS, LANES), F32),
-            pltpu.VMEM((SPAN + 4, rows, LANES), F32),
+            pltpu.VMEM((n_tmpl, rows, LANES), F32),
             pltpu.VMEM((rows, depth), F32),
             pltpu.VMEM((rows // 8, 8 * STEP, depth), BF16),
             pltpu.VMEM((SPAN + 2, rows // 8, 8 * SUB, LANES), BF16),
@@ -280,7 +287,7 @@
             pltpu.VMEM((blocks, GROUPS, LANES), BF16),
             pltpu.VMEM((n_sta, blocks // n_sta, GROUPS, LANES), BF16),
             pltpu.VMEM((8, LANES), jnp.int32),
-            pltpu.SemaphoreType.DMA,
+            pltpu.SemaphoreType.DMA((LIB_COPIES,)),
             pltpu.SemaphoreType.DMA,
             pltpu.SemaphoreType.DMA,
             pltpu.SemaphoreType.DMA,

time: 15.5 us -> 15.5 us (level)
  no operation moved by 1% of the time
where the time goes in v4:
time: 15.5 us; the launch traced here: 15.4 us
  Pallas kernels  14.1 us (91%)
  between operations  0.66 us (4%)
  local copies, waits for them, and re-layouts  0.6 us (4%)
    pallas_call x1, Pallas kernels, on_device(): pl.pallas_call(functools.partial(kernel, n_tmpl, n_sta, chans, length, ro...  14.1 us
    unnamed x1, local copies, waits for them, and re-layouts  0.6 us

profile of v4, /device:TPU:0, one launch (start us, length us, event | category | flops | bytes accessed | tf_op | source)
XLA Modules:
  0.0 15.4 jit_solution(16930399337259835008)
XLA Ops:
  0.7 14.1 %shard_map.55 = bf16[1,16,128]{2,1,0:T(8,128)(2,1)S(1)} custom-call(bf16[75,128]{1,0:T(8,128)(2,1)} %win_ref.1, bf16[75,4,16,300]{3,2,1,0:T(8,128)(2,1)} %bitcast.4, s32[1]{0:T(128)S(6)} %copy.8.index_ref, s32[1,75]{1,0:T(1,128)} %move_ref.1, s32[1,75]{1,0:T(1,128)} %bitcast.5), custom_call_target="tpu_custom_call" | custom-call | tf_op jit(solution)/shard_map/pallas_call | solution.py:264
  14.8 0.6 %copy.7 = bf16[1,16,128]{2,1,0:T(8,128)(2,1)} copy(bf16[1,16,128]{2,1,0:T(8,128)(2,1)S(1)} %shard_map.55) | data formatting | bytes 8192
